TPU v7x, 512 devices: a whole 4x4x16 slice. The times are simulated.
512 devices in a mesh: queue: 32 (over z, y_hi), tensor: 16 (over x, y_lo, core).
Axes of the slice: x: 4, y: 4 (y_hi: 2, y_lo: 2; y = y_hi * 2 + y_lo), z: 16, core: 2. Of those that a mesh axis runs over, the one named last changes fastest.
Arguments:
- frames_in: bfloat16 [32, 384, 3072], P('queue', None, 'tensor'), may hold values from -6 to 6
- fresh: bfloat16 [384, 3072], P(None, 'tensor'), may hold values from -6 to 6
- levels: int32 [32], P('queue'), may hold values from 0 to 127, as said below
- reach: int32 [32], P('queue'), may hold values from 0 to 3
- level_mod: bfloat16 [128, 3, 3072], P(None, None, 'tensor'), may hold values from -3 to 3
- w_qkv: bfloat16 [3072, 3, 2048], P(None, None, 'tensor')
- q_gain: float32 [2048], P('tensor'), as said below
- k_gain: float32 [2048], P('tensor'), as said below
- w_out: bfloat16 [2048, 3072], P('tensor'), may hold values from -0.75 to 0.75
Outputs:
- frames_out: bfloat16 [32, 384, 3072], P('queue', None, 'tensor')
Inputs may be any that keep to these rules, and one draw needn't show every extreme that they name: levels[f] lies in [f * 4, (f + 1) * 4), so levels rise with the slot. `q_gain`: positive. `k_gain`: positive.
All inputs are finite; a program needn't handle non-finite values.
Results may differ from a plain program's by a relative error of at most 0.008.
The roundings to bfloat16 on the way count: a program that leaves them out, or rounds other values in their place, can miss the bound.
Values may be sent and summed in bfloat16 or wider, within the bound.
A program may use at most 64 MiB of HBM per device.

v0:
```python
import jax
import jax.numpy as jnp
from jax import lax
from jax.sharding import PartitionSpec as P

HD = 128
REACH = 3


EPS = 1e-06


def passed_along(value, axis, steps):
    count = lax.axis_size(axis)
    first, last = (max(0, -steps), min(count, count - steps))
    return lax.ppermute(value, axis, [(source, source + steps) for source in range(first, last)])


def rms_gain(values, gain):
    power = jnp.mean(values * values, axis=-1, keepdims=True)
    return values * lax.rsqrt(power + EPS) * gain


def local(frames_in, fresh, levels, reach, level_mod, w_qkv, q_gain, k_gain, w_out):
    queue_pos = lax.axis_index("queue")
    slot_count = lax.axis_size("queue")
    moved = passed_along(frames_in, "queue", 1)[0]
    current = jnp.where(queue_pos == 0, fresh, moved)
    level_count = level_mod.shape[0]
    chosen = jnp.arange(level_count, dtype=jnp.int32) == levels[0]
    picked = jnp.sum(jnp.where(chosen[:, None, None], level_mod.astype(jnp.float32), 0.0), axis=0)
    width = w_qkv.shape[2]
    model_width = w_qkv.shape[0]
    heads_local = width // HD
    tokens = current.shape[0]
    flat_weight = w_qkv.reshape(model_width, 3 * width)
    picked_half = picked.astype(jnp.bfloat16)
    whole, mod_whole = (
        lax.all_gather(current, "tensor", axis=1, tiled=True),
        lax.all_gather(picked_half[:2], "tensor", axis=1, tiled=True),
    )
    latent = whole.astype(jnp.float32)
    mod_full = mod_whole.astype(jnp.float32)
    center = jnp.mean(latent, axis=-1, keepdims=True)
    spread = jnp.mean((latent - center) ** 2, axis=-1, keepdims=True)
    normed = (latent - center) * lax.rsqrt(spread + EPS)
    hidden = (normed * (1.0 + mod_full[1][None, :]) + mod_full[0][None, :]).astype(jnp.bfloat16)
    packed = jnp.dot(hidden, flat_weight, preferred_element_type=jnp.float32)
    packed = packed.reshape(tokens, 3, heads_local, HD)
    query = rms_gain(packed[:, 0], q_gain.reshape(heads_local, HD)).astype(jnp.bfloat16)
    keyed = rms_gain(packed[:, 1], k_gain.reshape(heads_local, HD)).astype(jnp.bfloat16)
    valued = packed[:, 2].astype(jnp.bfloat16)
    offsets = [0]
    key_list = [keyed]
    value_list = [valued]
    for distance in range(1, REACH + 1):
        for direction in (1, -1):
            got_keys, got_values = passed_along((keyed, valued), "queue", direction * distance)
            offsets.append(-direction * distance)
            key_list.append(got_keys)
            value_list.append(got_values)
    all_keys = jnp.stack(key_list, axis=0)
    all_values = jnp.stack(value_list, axis=0)
    offset_array = jnp.array(offsets, dtype=jnp.int32)
    target = queue_pos + offset_array
    usable = (jnp.abs(offset_array) <= reach[0]) & (target >= 0) & (target < slot_count)

    def one_head(head):
        head_rows = lax.dynamic_index_in_dim(query, head, 1, keepdims=False)
        head_keys = lax.dynamic_index_in_dim(all_keys, head, 2, keepdims=False)
        head_values = lax.dynamic_index_in_dim(all_values, head, 2, keepdims=False)
        scores = jnp.einsum(
            "td,psd->tps", head_rows, head_keys, preferred_element_type=jnp.float32
        ) * HD ** (-0.5)
        scores = jnp.where(usable[None, :, None], scores, -jnp.inf)
        highest = jnp.max(scores, axis=(1, 2), keepdims=True)
        expd = jnp.exp(scores - highest)
        weights = (expd / jnp.sum(expd, axis=(1, 2), keepdims=True)).astype(jnp.bfloat16)
        mixed = jnp.einsum("tps,psd->td", weights, head_values, preferred_element_type=jnp.float32)
        return mixed.astype(jnp.bfloat16)

    per_head = lax.map(one_head, jnp.arange(heads_local, dtype=jnp.int32))
    attn = jnp.transpose(per_head, (1, 0, 2)).reshape(tokens, width)
    columns = lax.all_to_all(w_out, "tensor", split_axis=1, concat_axis=0, tiled=True)
    head_rows = columns
    proj = jnp.dot(
        lax.all_gather(attn, "tensor", axis=1, tiled=True),
        head_rows,
        preferred_element_type=jnp.float32,
    )
    gate_row = picked[2][None, :]
    result = current.astype(jnp.float32) + gate_row * proj
    return result.astype(jnp.bfloat16)[None]


def solution(mesh):
    return jax.shard_map(
        local,
        mesh=mesh,
        in_specs=(
            P("queue", None, "tensor"),
            P(None, "tensor"),
            P("queue"),
            P("queue"),
            P(None, None, "tensor"),
            P(None, None, "tensor"),
            P("tensor"),
            P("tensor"),
            P("tensor", None),
        ),
        out_specs=P("queue", None, "tensor"),
        check_vma=False,
    )
```

profile of v0, /device:TPU:1, one launch (start us, length us, event | category | flops | bytes accessed | tf_op | source)
XLA Modules:
  0.0 211.4 jit_solution(12947911352076166225)
XLA Ops:
  6.5 5.8 %collective-permute-start = (bf16[1,384,192]{1,2,0:T(8,128)(2,1)}, bf16[1,384,192]{1,2,0:T(8,128)(2,1)S(1)}, u32[]{:S(2)}, u32[]{:S(2)}) collective-permute-start(bf16[1,384,192]{1,2,0:T(8,128)(2,1)} %param.10), channel_id=1, source_target_pairs={{0,16},{16,32},{32,48},{48,64},{64,80},{80,96},{96,112},{112,128},... | collective-permute-start | bytes 442376 | tf_op jit(solution)/shard_map/ppermute | solution.py:16
  12.3 2.4 %collective-permute-done = bf16[1,384,192]{1,2,0:T(8,128)(2,1)S(1)} collective-permute-done((bf16[1,384,192]{1,2,0:T(8,128)(2,1)}, bf16[1,384,192]{1,2,0:T(8,128)(2,1)S(1)}, u32[]{:S(2)}, u32[]{:S(2)}) %collective-permute-start) | collective-permute-done | bytes 147488 | tf_op jit(solution)/shard_map/ppermute | solution.py:16
  14.7 1.6 bitcast_select_fusion
  16.3 0.0 all-gather.4.cloned.1.call-update
  16.3 0.0 all-gather.6.cloned.1.call-start
  17.0 1.1 select_reduce_fusion
  18.1 20.6 %all-gather = bf16[16,192,2]{1,2,0:T(2,128)(2,1)S(1)} all-gather(bf16[1,192,2]{1,2,0:T(2,128)(2,1)S(1)} %fusion.42), channel_id=1, replica_groups=mesh['queue'=32,'tensor'=16] {'tensor'}, dimensions={0}, use_global_device_ids=true | all-gather | bytes 13056 | tf_op jit(solution)/shard_map/all_gather | solution.py:40
  38.7 0.1 reshape.242
  38.8 2.9 %copy.39 = bf16[3072,3,128]{0,2,1:T(8,128)(2,1)S(1)} copy(bf16[3072,3,128]{2,0,1:T(8,128)(2,1)} %param.15) | data formatting | bytes 4718592 | tf_op args[5]
  42.4 22.5 %all-gather.4.cloned.1.call-done = bf16[384,3072]{0,1:T(8,128)(2,1)} async-done(((bf16[384,192]{0,1:T(8,128)(2,1)}), bf16[384,3072]{0,1:T(8,128)(2,1)}) %all-gather.4.cloned.1.call-update) | async-done | bytes 2359312 | tf_op jit(solution)/shard_map/all_gather | solution.py:39
  65.0 2.3 %convert_reduce_fusion = f32[384]{0:T(512)S(1)} fusion(bf16[384,3072]{0,1:T(8,128)(2,1)} %all-gather.4.cloned.1.call-done), kind=kLoop, calls=%fused_computation.1 | loop fusion | flops 2358912 | bytes 2360832 | tf_op jit(solution)/shard_map/reduce_sum | solution.py:44
  67.2 2.4 %fusion.2 = f32[384]{0:T(512)S(1)} fusion(bf16[384,3072]{0,1:T(8,128)(2,1)} %all-gather.4.cloned.1.call-done, f32[384]{0:T(512)S(1)} %broadcast_multiply_fusion), kind=kLoop, calls=%fused_computation.4 | loop fusion | flops 4718208 | bytes 2362368 | tf_op jit(solution)/shard_map/reduce_sum | solution.py:45
  69.6 0.0 copy-start.3
  69.6 0.0 copy-start.4
  69.6 1.6 fusion.16
  71.3 4.3 %collective-permute-start.7 = (bf16[384,1,128]{0,2,1:T(8,128)(2,1)S(1)}, bf16[384,1,128]{0,2,1:T(8,128)(2,1)S(1)}, u32[]{:S(2)}, u32[]{:S(2)}) collective-permute-start(bf16[384,1,128]{0,2,1:T(8,128)(2,1)S(1)} %fusion.41), channel_id=1, source_target_pairs={{0,16},{16,32},{32,48},{48,64},{64,80},{80,96},{96,112},{112,128},... | collective-permute-start | bytes 294920 | tf_op jit(solution)/shard_map/ppermute | solution.py:16
  75.6 1.3 collective-permute-start.8
  76.9 5.3 %collective-permute-start.9 = (bf16[384,1,128]{0,2,1:T(8,128)(2,1)S(1)}, bf16[384,1,128]{0,2,1:T(8,128)(2,1)S(1)}, u32[]{:S(2)}, u32[]{:S(2)}) collective-permute-start(bf16[384,1,128]{0,2,1:T(8,128)(2,1)S(1)} %fusion.41), channel_id=1, source_target_pairs={{0,32},{16,48},{32,64},{48,80},{64,96},{80,112},{96,128},{112,144}... | collective-permute-start | bytes 294920 | tf_op jit(solution)/shard_map/ppermute | solution.py:16
  82.2 1.3 collective-permute-start.10
  83.5 0.1 bitcast_dynamic-update-slice_fusion.6
  83.6 0.1 fusion.30
  83.7 3.4 %collective-permute-start.1 = (bf16[384,1,128]{0,2,1:T(8,128)(2,1)S(1)}, bf16[384,1,128]{0,2,1:T(8,128)(2,1)S(1)}, u32[]{:S(2)}, u32[]{:S(2)}) collective-permute-start(bf16[384,1,128]{0,2,1:T(8,128)(2,1)S(1)} %fusion.30), channel_id=1, source_target_pairs={{0,16},{16,32},{32,48},{48,64},{64,80},{80,96},{96,112},{112,128},... | collective-permute-start | bytes 294920 | tf_op jit(solution)/shard_map/ppermute | solution.py:16
  87.1 1.6 collective-permute-done.1
  88.8 1.3 collective-permute-start.2
  90.1 5.9 %collective-permute-done.2 = bf16[384,1,128]{0,2,1:T(8,128)(2,1)S(1)} collective-permute-done((bf16[384,1,128]{0,2,1:T(8,128)(2,1)S(1)}, bf16[384,1,128]{0,2,1:T(8,128)(2,1)S(1)}, u32[]{:S(2)}, u32[]{:S(2)}) %collective-permute-start.2) | collective-permute-done | bytes 98336 | tf_op jit(solution)/shard_map/ppermute | solution.py:16
  96.0 6.4 %collective-permute-start.3 = (bf16[384,1,128]{0,2,1:T(8,128)(2,1)S(1)}, bf16[384,1,128]{0,2,1:T(8,128)(2,1)S(1)}, u32[]{:S(2)}, u32[]{:S(2)}) collective-permute-start(bf16[384,1,128]{0,2,1:T(8,128)(2,1)S(1)} %fusion.30), channel_id=1, source_target_pairs={{0,32},{16,48},{32,64},{48,80},{64,96},{80,112},{96,128},{112,144}... | collective-permute-start | bytes 294920 | tf_op jit(solution)/shard_map/ppermute | solution.py:16
  102.4 1.6 collective-permute-done.3
  104.0 1.3 collective-permute-start.4
  105.3 4.4 %collective-permute-done.4 = bf16[384,1,128]{0,2,1:T(8,128)(2,1)S(1)} collective-permute-done((bf16[384,1,128]{0,2,1:T(8,128)(2,1)S(1)}, bf16[384,1,128]{0,2,1:T(8,128)(2,1)S(1)}, u32[]{:S(2)}, u32[]{:S(2)}) %collective-permute-start.4) | collective-permute-done | bytes 98336 | tf_op jit(solution)/shard_map/ppermute | solution.py:16
  109.7 8.0 %collective-permute-start.5 = (bf16[384,1,128]{0,2,1:T(8,128)(2,1)S(1)}, bf16[384,1,128]{0,2,1:T(8,128)(2,1)S(1)}, u32[]{:S(2)}, u32[]{:S(2)}) collective-permute-start(bf16[384,1,128]{0,2,1:T(8,128)(2,1)S(1)} %fusion.30), channel_id=1, source_target_pairs={{0,48},{16,64},{32,80},{48,96},{64,112},{80,128},{96,144},{112,160... | collective-permute-start | bytes 294920 | tf_op jit(solution)/shard_map/ppermute | solution.py:16
  117.7 1.6 collective-permute-done.5
  119.3 1.3 collective-permute-start.6
  120.6 8.3 %collective-permute-done.6 = bf16[384,1,128]{0,2,1:T(8,128)(2,1)S(1)} collective-permute-done((bf16[384,1,128]{0,2,1:T(8,128)(2,1)S(1)}, bf16[384,1,128]{0,2,1:T(8,128)(2,1)S(1)}, u32[]{:S(2)}, u32[]{:S(2)}) %collective-permute-start.6) | collective-permute-done | bytes 98336 | tf_op jit(solution)/shard_map/ppermute | solution.py:16
  128.9 7.1 %collective-permute-start.11 = (bf16[384,1,128]{0,2,1:T(8,128)(2,1)S(1)}, bf16[384,1,128]{0,2,1:T(8,128)(2,1)S(1)}, u32[]{:S(2)}, u32[]{:S(2)}) collective-permute-start(bf16[384,1,128]{0,2,1:T(8,128)(2,1)S(1)} %fusion.41), channel_id=1, source_target_pairs={{0,48},{16,64},{32,80},{48,96},{64,112},{80,128},{96,144},{112,160... | collective-permute-start | bytes 294920 | tf_op jit(solution)/shard_map/ppermute | solution.py:16
  136.1 0.9 fusion.6
  137.0 0.9 fusion.7
  137.9 0.0 collective-permute-done.7
  137.9 1.3 collective-permute-start.12
  139.4 7.5 %collective-permute-done.12 = bf16[384,1,128]{0,2,1:T(8,128)(2,1)S(1)} collective-permute-done((bf16[384,1,128]{0,2,1:T(8,128)(2,1)S(1)}, bf16[384,1,128]{0,2,1:T(8,128)(2,1)S(1)}, u32[]{:S(2)}, u32[]{:S(2)}) %collective-permute-start.12) | collective-permute-done | bytes 98336 | tf_op jit(solution)/shard_map/ppermute | solution.py:16
  146.9 0.0 copy-start.1
  146.9 0.0 copy-start.2
  146.9 1.9 fusion.22
  148.8 0.0 all-gather.6.cloned.1.call-update
  148.8 1.1 copy.45
  150.0 13.0 %all-to-all-start = ((bf16[128,16,192]{0,2,1:T(8,128)(2,1)}), bf16[128,16,192]{0,2,1:T(8,128)(2,1)S(1)}, u32[]{:S(2)}, u32[]{:S(2)}) async-start(bf16[128,16,192]{0,2,1:T(8,128)(2,1)} %bitcast.35), calls=%async_computation | async-start | bytes 1572864 | tf_op jit(solution)/shard_map/all_to_all | solution.py:84
  163.0 12.6 %all-to-all-done = bf16[128,16,192]{0,2,1:T(8,128)(2,1)S(1)} async-done(((bf16[128,16,192]{0,2,1:T(8,128)(2,1)}), bf16[128,16,192]{0,2,1:T(8,128)(2,1)S(1)}, u32[]{:S(2)}, u32[]{:S(2)}) %all-to-all-start) | async-done | bytes 786464 | tf_op jit(solution)/shard_map/all_to_all | solution.py:84
  175.6 26.2 %all-gather.6.cloned.1.call-done = bf16[384,2048]{1,0:T(8,128)(2,1)} async-done(((bf16[384,128]{1,0:T(8,128)(2,1)}), bf16[384,2048]{1,0:T(8,128)(2,1)}) %all-gather.6.cloned.1.call-update) | async-done | bytes 1572880 | tf_op jit(solution)/shard_map/all_gather | solution.py:87
  201.8 2.7 %fusion.33 = bf16[1,384,192]{1,2,0:T(8,128)(2,1)} fusion(bf16[384,192]{0,1:T(8,128)(2,1)S(1)} %copy-done.2, bf16[384,2048]{1,0:T(8,128)(2,1)} %all-gather.6.cloned.1.call-done, f32[192]{0:T(256)S(1)} %bitcast.113, bf16[128,16,192]{0,2,1:T(8,128)(2,1)S(1)} %all-to-all-done), kind=kOutput, calls=%fused_computation.42 | convolution fusion | flops 302284800 | bytes 2654976 | tf_op jit(solution)/shard_map/dot_general | solution.py:86
  (40 shorter events, 0.4 us)
Async XLA Ops:
  6.5 35.8 %copy-start.5 = (s32[7]{0:T(128)S(1)}, s32[7]{0:T(128)}, u32[]{:S(2)}) copy-start(s32[7]{0:T(128)} %constant.55.clone) | copy-start | bytes 88
  6.5 35.8 %copy-start.6 = (s32[7]{0:T(128)S(1)}, s32[7]{0:T(128)}, u32[]{:S(2)}) copy-start(s32[7]{0:T(128)} %constant.59) | copy-start | bytes 88
  6.5 58.4 %all-gather.4.cloned.1.call-start = ((), (), s32[]{:S(2)}) async-start(), calls=%async_computation.1 | async-start | bytes 2506752 | tf_op jit(solution)/shard_map/all_gather | solution.py:39
  6.5 8.2 %collective-permute-start = (bf16[1,384,192]{1,2,0:T(8,128)(2,1)}, bf16[1,384,192]{1,2,0:T(8,128)(2,1)S(1)}, u32[]{:S(2)}, u32[]{:S(2)}) collective-permute-start(bf16[1,384,192]{1,2,0:T(8,128)(2,1)} %param.10), channel_id=1, source_target_pairs={{0,16},{16,32},{32,48},{48,64},{64,80},{80,96},{96,112},{112,128},... | collective-permute-start | bytes 442376 | tf_op jit(solution)/shard_map/ppermute | solution.py:16
  16.3 185.5 %all-gather.6.cloned.1.call-start = ((), (), s32[]{:S(2)}) async-start(), calls=%async_computation.2 | async-start | bytes 1671168 | tf_op jit(solution)/shard_map/all_gather | solution.py:87
  65.0 4.6 %copy-start = (bf16[384,3072]{0,1:T(8,128)(2,1)S(1)}, bf16[384,3072]{0,1:T(8,128)(2,1)}, u32[]{:S(2)}) copy-start(bf16[384,3072]{0,1:T(8,128)(2,1)} %all-gather.4.cloned.1.call-done) | copy-start | bytes 7077892
  69.6 13.9 %copy-start.3 = (f32[128]{0:T(128)S(1)}, f32[128]{0:T(128)}, u32[]{:S(2)}) copy-start(f32[128]{0:T(128)} %param.17) | copy-start | bytes 1540
  69.6 66.5 %copy-start.4 = (f32[128]{0:T(128)S(1)}, f32[128]{0:T(128)}, u32[]{:S(2)}) copy-start(f32[128]{0:T(128)} %param.16) | copy-start | bytes 1540
  71.3 66.7 %collective-permute-start.7 = (bf16[384,1,128]{0,2,1:T(8,128)(2,1)S(1)}, bf16[384,1,128]{0,2,1:T(8,128)(2,1)S(1)}, u32[]{:S(2)}, u32[]{:S(2)}) collective-permute-start(bf16[384,1,128]{0,2,1:T(8,128)(2,1)S(1)} %fusion.41), channel_id=1, source_target_pairs={{0,16},{16,32},{32,48},{48,64},{64,80},{80,96},{96,112},{112,128},... | collective-permute-start | bytes 294920 | tf_op jit(solution)/shard_map/ppermute | solution.py:16
  75.6 63.7 %collective-permute-start.8 = (bf16[384,1,128]{0,2,1:T(8,128)(2,1)S(1)}, bf16[384,1,128]{0,2,1:T(8,128)(2,1)S(1)}, u32[]{:S(2)}, u32[]{:S(2)}) collective-permute-start(bf16[384,1,128]{0,2,1:T(8,128)(2,1)S(1)} %fusion.41), channel_id=1, source_target_pairs={{16,0},{32,16},{48,32},{64,48},{80,64},{96,80},{112,96},{128,112},... | collective-permute-start | bytes 294920 | tf_op jit(solution)/shard_map/ppermute | solution.py:16
  76.9 62.4 %collective-permute-start.9 = (bf16[384,1,128]{0,2,1:T(8,128)(2,1)S(1)}, bf16[384,1,128]{0,2,1:T(8,128)(2,1)S(1)}, u32[]{:S(2)}, u32[]{:S(2)}) collective-permute-start(bf16[384,1,128]{0,2,1:T(8,128)(2,1)S(1)} %fusion.41), channel_id=1, source_target_pairs={{0,32},{16,48},{32,64},{48,80},{64,96},{80,112},{96,128},{112,144}... | collective-permute-start | bytes 294920 | tf_op jit(solution)/shard_map/ppermute | solution.py:16
  82.2 57.1 %collective-permute-start.10 = (bf16[384,1,128]{0,2,1:T(8,128)(2,1)S(1)}, bf16[384,1,128]{0,2,1:T(8,128)(2,1)S(1)}, u32[]{:S(2)}, u32[]{:S(2)}) collective-permute-start(bf16[384,1,128]{0,2,1:T(8,128)(2,1)S(1)} %fusion.41), channel_id=1, source_target_pairs={{32,0},{48,16},{64,32},{80,48},{96,64},{112,80},{128,96},{144,112}... | collective-permute-start | bytes 294920 | tf_op jit(solution)/shard_map/ppermute | solution.py:16
  83.7 5.0 %collective-permute-start.1 = (bf16[384,1,128]{0,2,1:T(8,128)(2,1)S(1)}, bf16[384,1,128]{0,2,1:T(8,128)(2,1)S(1)}, u32[]{:S(2)}, u32[]{:S(2)}) collective-permute-start(bf16[384,1,128]{0,2,1:T(8,128)(2,1)S(1)} %fusion.30), channel_id=1, source_target_pairs={{0,16},{16,32},{32,48},{48,64},{64,80},{80,96},{96,112},{112,128},... | collective-permute-start | bytes 294920 | tf_op jit(solution)/shard_map/ppermute | solution.py:16
  88.8 7.2 %collective-permute-start.2 = (bf16[384,1,128]{0,2,1:T(8,128)(2,1)S(1)}, bf16[384,1,128]{0,2,1:T(8,128)(2,1)S(1)}, u32[]{:S(2)}, u32[]{:S(2)}) collective-permute-start(bf16[384,1,128]{0,2,1:T(8,128)(2,1)S(1)} %fusion.30), channel_id=1, source_target_pairs={{16,0},{32,16},{48,32},{64,48},{80,64},{96,80},{112,96},{128,112},... | collective-permute-start | bytes 294920 | tf_op jit(solution)/shard_map/ppermute | solution.py:16
  96.0 8.0 %collective-permute-start.3 = (bf16[384,1,128]{0,2,1:T(8,128)(2,1)S(1)}, bf16[384,1,128]{0,2,1:T(8,128)(2,1)S(1)}, u32[]{:S(2)}, u32[]{:S(2)}) collective-permute-start(bf16[384,1,128]{0,2,1:T(8,128)(2,1)S(1)} %fusion.30), channel_id=1, source_target_pairs={{0,32},{16,48},{32,64},{48,80},{64,96},{80,112},{96,128},{112,144}... | collective-permute-start | bytes 294920 | tf_op jit(solution)/shard_map/ppermute | solution.py:16
  104.0 5.7 %collective-permute-start.4 = (bf16[384,1,128]{0,2,1:T(8,128)(2,1)S(1)}, bf16[384,1,128]{0,2,1:T(8,128)(2,1)S(1)}, u32[]{:S(2)}, u32[]{:S(2)}) collective-permute-start(bf16[384,1,128]{0,2,1:T(8,128)(2,1)S(1)} %fusion.30), channel_id=1, source_target_pairs={{32,0},{48,16},{64,32},{80,48},{96,64},{112,80},{128,96},{144,112}... | collective-permute-start | bytes 294920 | tf_op jit(solution)/shard_map/ppermute | solution.py:16
  109.7 9.6 %collective-permute-start.5 = (bf16[384,1,128]{0,2,1:T(8,128)(2,1)S(1)}, bf16[384,1,128]{0,2,1:T(8,128)(2,1)S(1)}, u32[]{:S(2)}, u32[]{:S(2)}) collective-permute-start(bf16[384,1,128]{0,2,1:T(8,128)(2,1)S(1)} %fusion.30), channel_id=1, source_target_pairs={{0,48},{16,64},{32,80},{48,96},{64,112},{80,128},{96,144},{112,160... | collective-permute-start | bytes 294920 | tf_op jit(solution)/shard_map/ppermute | solution.py:16
  119.3 9.6 %collective-permute-start.6 = (bf16[384,1,128]{0,2,1:T(8,128)(2,1)S(1)}, bf16[384,1,128]{0,2,1:T(8,128)(2,1)S(1)}, u32[]{:S(2)}, u32[]{:S(2)}) collective-permute-start(bf16[384,1,128]{0,2,1:T(8,128)(2,1)S(1)} %fusion.30), channel_id=1, source_target_pairs={{48,0},{64,16},{80,32},{96,48},{112,64},{128,80},{144,96},{160,112... | collective-permute-start | bytes 294920 | tf_op jit(solution)/shard_map/ppermute | solution.py:16
  128.9 10.4 %collective-permute-start.11 = (bf16[384,1,128]{0,2,1:T(8,128)(2,1)S(1)}, bf16[384,1,128]{0,2,1:T(8,128)(2,1)S(1)}, u32[]{:S(2)}, u32[]{:S(2)}) collective-permute-start(bf16[384,1,128]{0,2,1:T(8,128)(2,1)S(1)} %fusion.41), channel_id=1, source_target_pairs={{0,48},{16,64},{32,80},{48,96},{64,112},{80,128},{96,144},{112,160... | collective-permute-start | bytes 294920 | tf_op jit(solution)/shard_map/ppermute | solution.py:16
  137.9 9.0 %collective-permute-start.12 = (bf16[384,1,128]{0,2,1:T(8,128)(2,1)S(1)}, bf16[384,1,128]{0,2,1:T(8,128)(2,1)S(1)}, u32[]{:S(2)}, u32[]{:S(2)}) collective-permute-start(bf16[384,1,128]{0,2,1:T(8,128)(2,1)S(1)} %fusion.41), channel_id=1, source_target_pairs={{48,0},{64,16},{80,32},{96,48},{112,64},{128,80},{144,96},{160,112... | collective-permute-start | bytes 294920 | tf_op jit(solution)/shard_map/ppermute | solution.py:16
  146.9 1.9 copy-start.1
  146.9 54.9 %copy-start.2 = (bf16[384,192]{0,1:T(8,128)(2,1)S(1)}, bf16[384,192]{0,1:T(8,128)(2,1)}, u32[]{:S(2)}) copy-start(bf16[384,192]{0,1:T(8,128)(2,1)} %bitcast_select_fusion) | copy-start | bytes 442372
  150.0 25.6 %all-to-all-start = ((bf16[128,16,192]{0,2,1:T(8,128)(2,1)}), bf16[128,16,192]{0,2,1:T(8,128)(2,1)S(1)}, u32[]{:S(2)}, u32[]{:S(2)}) async-start(bf16[128,16,192]{0,2,1:T(8,128)(2,1)} %bitcast.35), calls=%async_computation | async-start | bytes 1572864 | tf_op jit(solution)/shard_map/all_to_all | solution.py:84
Sparse Core Ops, SparseCore 0:
  16.5 48.4 all-gather.3
  149.0 52.8 all-gather.5
where the time goes:
time: 212 us; the launch traced here: 211 us
  waiting for transfers between devices  94.7 us (45%)
  starting transfers between devices  61 us (29%)
  blocking collectives  20.6 us (10%)
  between operations  15.1 us (7%)
  other arithmetic  8.53 us (4%)
  matrix products  7.06 us (3%)
  local copies, waits for them, and re-layouts  4.46 us (2%)
    ppermute x13, starting transfers between devices, passed_along(): lax.ppermute(value, axis, [(source, source + steps) for source in range(f...  48 us
    ppermute x13, waiting for transfers between devices, passed_along(): lax.ppermute(value, axis, [(source, source + steps) for source in range(f...  33.3 us
    all_gather x1, waiting for transfers between devices, local(): lax.all_gather(attn, 'tensor', axis=1, tiled=True)  26.2 us
    all_gather x1, waiting for transfers between devices, local(): lax.all_gather(current, 'tensor', axis=1, tiled=True)  22.5 us
    all_gather x1, blocking collectives, local(): lax.all_gather(picked_half[:2], 'tensor', axis=1, tiled=True)  20.6 us
    all_to_all x1, starting transfers between devices, local(): lax.all_to_all(w_out, 'tensor', split_axis=1, concat_axis=0, tiled=True)  13 us
    all_to_all x1, waiting for transfers between devices, local(): lax.all_to_all(w_out, 'tensor', split_axis=1, concat_axis=0, tiled=True)  12.6 us
    unnamed x27, local copies, waits for them, and re-layouts  4.31 us
  transfers between devices with their start and end apart: 16, of which 11 were waited for; matrix products, arithmetic and copies ran while one was open for 4% of the time, Pallas kernels for 0%

commit v1 on v0

v1 whole, which is shorter than its diff:
```python
import jax
import jax.numpy as jnp
from jax import lax
from jax.experimental import pallas as pl
from jax.experimental.pallas import tpu as pltpu
from jax.sharding import PartitionSpec as P

MESH = pl.DeviceIdType.MESH
HD = 128
EPS = 1e-06
LANE = 128
F32 = jnp.float32
BF16 = jnp.bfloat16


def kernel(
    queues, levels_ref, reach_ref, frames_ref, fresh_ref, mod_ref, w_ref, qg_ref, kg_ref, wo_ref,
    out_ref,
    xs, xr, st, stb, lm, modc, wq, wt, hb, qt, kv, m_s, l_s, o_s, ab, wo_in, wo_send, wo_recv, gains,
    local_sem, ss, r_shift, r_stat, r_h, r_kv, r_ab, r_wo,
):
    blocks = xs.shape[0]
    part = xs.shape[1]
    width = 16 * part
    q = lax.axis_index("queue")
    t = lax.axis_index("tensor")
    z, e = q // 2, q % 2
    x, y, c = t // 4, (t // 2) % 2, t % 2
    zs = queues // 2

    def tid(dx, fy, fc):
        xx = (x + dx) % 4
        yy = (y + fy) % 2
        cc = (c + fc) % 2
        return xx * 4 + yy * 2 + cc

    def queue_id(dz, flip):
        return ((z + dz + zs) % zs) * 2 + (e + flip) % 2

    sends = []

    def send(src, dst, recv_sem, device):
        copy = pltpu.make_async_remote_copy(
            src_ref=src, dst_ref=dst, send_sem=ss.at[len(sends)], recv_sem=recv_sem,
            device_id=device, device_id_type=MESH,
        )
        copy.start()
        sends.append(copy)

    def arrived(dst, recv_sem):
        pltpu.make_async_remote_copy(
            src_ref=dst, dst_ref=dst, send_sem=ss.at[0], recv_sem=recv_sem,
            device_id=(q, tid(0, 0, 1)), device_id_type=MESH,
        ).wait_recv()

    last = q == queues - 1
    loads = []

    def load(src, dst):
        copy = pltpu.make_async_copy(src, dst, local_sem.at[len(loads)])
        loads.append(copy)
        return copy

    for j in range(blocks):
        lanes = pl.ds(j * LANE, LANE)
        from_queue = load(frames_ref.at[:, lanes], xs.at[j])
        from_noise = pltpu.make_async_copy(fresh_ref.at[:, lanes], xs.at[j], local_sem.at[j])

        @pl.when(last)
        def _():
            from_noise.start()

        @pl.when(jnp.logical_not(last))
        def _():
            from_queue.start()

    load_mod = load(mod_ref, lm)
    load_w = load(w_ref, wq)
    load_wo = load(wo_ref, wo_in)
    load_qg = load(qg_ref, gains.at[pl.ds(0, 1)])
    load_kg = load(kg_ref, gains.at[pl.ds(8, 1)])
    for copy in (load_mod, load_w, load_wo, load_qg, load_kg):
        copy.start()

    after = (q + 1) % queues
    before = (q + queues - 1) % queues
    barrier = pltpu.get_barrier_semaphore()
    for k in range(1, 16):
        pl.semaphore_signal(barrier, inc=1, device_id=(q, (t + k) % 16), device_id_type=MESH)
    for k in range(16):
        pl.semaphore_signal(barrier, inc=1, device_id=(after, (t + k) % 16), device_id_type=MESH)
        pl.semaphore_signal(barrier, inc=1, device_id=(before, (t + k) % 16), device_id_type=MESH)
    for dz in (1, -1):
        pl.semaphore_signal(barrier, inc=1, device_id=(queue_id(dz, 0), t), device_id_type=MESH)

    for j in range(blocks):
        loads[j].wait()
        values = xs[j].astype(F32)
        total = jnp.sum(values, axis=0, keepdims=True)
        rest = values - total * (1.0 / part)
        st[j : j + 1, :] = total
        st[blocks + j : blocks + j + 1, :] = jnp.sum(rest * rest, axis=0, keepdims=True)
    pl.semaphore_wait(barrier, 15 + 32 + 2)

    send(xs.at[0], xr.at[0], r_shift.at[0], (after, t))
    for k in range(16):
        send(st, stb.at[t], r_stat.at[t], (after, (t + k) % 16))
    for j in range(1, blocks):
        send(xs.at[j], xr.at[j], r_shift.at[j], (after, t))

    load_mod.wait()
    chosen = lax.broadcasted_iota(jnp.int32, (part, LANE), 1) == levels_ref[0]
    for k in range(3):
        modc[k] = jnp.sum(jnp.where(chosen, lm[k].astype(F32), 0.0), axis=1, keepdims=True)
    load_qg.wait()
    load_kg.wait()
    eye = lax.broadcasted_iota(jnp.int32, (HD, HD), 0) == lax.broadcasted_iota(jnp.int32, (HD, HD), 1)
    q_gain = jnp.sum(jnp.where(eye, gains[0:1, :], 0.0), axis=1, keepdims=True)
    k_gain = jnp.sum(jnp.where(eye, gains[8:9, :], 0.0), axis=1, keepdims=True)

    load_w.wait()

    def turn(chip, _):
        for k in range(3):
            for piece in range(3):
                rows = pl.ds(pl.multiple_of(chip * 384 + piece * 128, 128), 128)
                wt[chip, k * 128 : (k + 1) * 128, piece * 128 : (piece + 1) * 128] = wq[k, rows, :].T
        return 0

    lax.fori_loop(0, 8, turn, 0)

    def slot_wait(j, slot):
        arrived(hb.at[j, slot], r_h.at[j, slot])

    def slot_send(j, slot, device_t):
        send(hb.at[j, slot], hb.at[j, slot], r_h.at[j, slot], (q, device_t))

    for k in range(16):
        slot = (t + k) % 16
        arrived(stb.at[slot], r_stat.at[slot])
    center = jnp.sum(stb[:, 0:blocks, :], axis=0) * (1.0 / width)
    offs = stb[:, 0:blocks, :] * (1.0 / part) - center[None]
    spread = jnp.sum(stb[:, blocks : 2 * blocks, :] + part * offs * offs, axis=0) * (1.0 / width)
    factor = lax.rsqrt(spread + EPS)

    def normalise(j):
        arrived(xr.at[j], r_shift.at[j])
        normed = (xr[j].astype(F32) - center[j : j + 1, :]) * factor[j : j + 1, :]
        hb[j, t] = (normed * (1.0 + modc[1]) + modc[0]).astype(BF16)
        for target in (tid(0, 1, 0), tid(2, 0, 0), tid(1, 0, 0), tid(3, 0, 0), tid(0, 0, 1)):
            slot_send(j, t, target)

    other = tid(0, 0, 1)

    def relay_y(j):
        slot = tid(0, 1, 0)
        slot_wait(j, slot)
        for target in (tid(1, 0, 0), tid(3, 0, 0), other):
            slot_send(j, slot, target)

    def relay_far(j):
        slot = tid(2, 0, 0)
        slot_wait(j, slot)
        slot_send(j, slot, tid(0, 1, 0))
        slot_send(j, slot, other)

    def relay_chip(j, dx, fy):
        slot = tid(dx, fy, 0)
        slot_wait(j, slot)
        slot_send(j, slot, other)

    def early(j):
        relay_y(j)
        relay_chip(j, 1, 0)
        relay_chip(j, 3, 0)
        relay_far(j)

    def late(j):
        relay_chip(j, 1, 1)
        relay_chip(j, 3, 1)
        relay_chip(j, 2, 1)

    sigma = 2 * e - 1
    own, s_near, s_away, o_0, o_near, o_away, o_far = range(7)

    def kv_send(j, slot, there, device):
        send(kv.at[slot, j], kv.at[there, j], r_kv.at[there, j], device)

    def kv_wait(j, slot):
        arrived(kv.at[slot, j], r_kv.at[slot, j])

    def project(j):
        for dx in range(4):
            for fy in range(2):
                slot = tid(dx, fy, 1)
                slot_wait(j, slot)

        def one(chip, total):
            h = hb[j, pl.ds(2 * chip, 2)].reshape(2 * part, LANE)
            return total + jnp.dot(wt[chip], h, preferred_element_type=F32)

        packed = lax.fori_loop(0, 8, one, jnp.zeros((3 * HD, LANE), F32))
        query, keyed, valued = packed[:HD], packed[HD : 2 * HD], packed[2 * HD :]

        def rms(values, gain):
            power = jnp.mean(values * values, axis=0, keepdims=True)
            return (values * lax.rsqrt(power + EPS) * gain).astype(BF16)

        kv[own, j, 0] = rms(keyed, k_gain).T
        kv[own, j, 1] = valued.astype(BF16)
        kv_send(j, own, s_near, (queue_id(sigma, 0), t))
        kv_send(j, own, o_0, (queue_id(0, 1), t))
        kv_send(j, own, s_away, (queue_id(-sigma, 0), t))
        qt[:, j * LANE : (j + 1) * LANE] = rms(query, q_gain)

    def kv_relay_1(j):
        kv_wait(j, s_near)
        kv_send(j, s_near, o_near, (queue_id(0, 1), t))
        kv_wait(j, o_0)
        kv_send(j, o_0, o_away, (queue_id(sigma, 0), t))

    def kv_relay_2(j):
        kv_wait(j, o_near)
        kv_send(j, o_near, o_far, (queue_id(-sigma, 0), t))

    normalise(0)
    normalise(1)
    early(0)
    normalise(2)
    early(1)
    late(0)
    project(0)
    early(2)
    late(1)
    project(1)
    kv_relay_1(0)
    late(2)
    project(2)

    load_wo.wait()

    def turn_out(k, _):
        lanes = pl.ds(pl.multiple_of(k * 384, 128), 384)
        wo_send[pl.ds(2 * k, 2)] = wo_in[:, lanes].T.reshape(2, part, LANE)
        return 0

    lax.fori_loop(0, 8, turn_out, 0)
    for k in range(1, 16):
        target = (t + k) % 16
        send(wo_send.at[target], wo_recv.at[t], r_wo.at[t], (q, target))

    f = q
    scale = HD ** (-0.5)
    m_s[...] = jnp.full(m_s.shape, -jnp.inf, F32)
    l_s[...] = jnp.zeros(l_s.shape, F32)
    o_s[...] = jnp.zeros(o_s.shape, F32)

    def attend(slot, offset):
        keys = kv[slot, :, 0].reshape(blocks * LANE, HD)
        scores = jnp.dot(keys, qt[...], preferred_element_type=F32)
        frame = f + offset
        usable = (jnp.abs(offset) <= reach_ref[0]) & (frame >= 0) & (frame < queues)
        scores = scores * scale + jnp.where(usable, 0.0, -jnp.inf).astype(F32)
        m_old = m_s[0:1, :]
        m_new = jnp.maximum(m_old, jnp.max(scores, axis=0, keepdims=True))
        weights = jnp.exp(scores - m_new)
        fade = jnp.exp(m_old - m_new)
        l_s[0:1, :] = l_s[0:1, :] * fade + jnp.sum(weights, axis=0, keepdims=True)
        m_s[0:1, :] = m_new
        half = weights.astype(BF16)
        values = jnp.concatenate([kv[slot, j, 1] for j in range(blocks)], axis=1)
        o_s[...] = o_s[...] * fade + jnp.dot(values, half, preferred_element_type=F32)

    kv_relay_1(1)
    kv_relay_2(0)
    attend(own, 0)
    kv_relay_1(2)
    kv_relay_2(1)
    attend(s_near, -2 * sigma)
    attend(o_0, -sigma)
    kv_relay_2(2)
    attend(o_near, sigma)
    for j in range(blocks):
        kv_wait(j, s_away)
    attend(s_away, 2 * sigma)
    for j in range(blocks):
        kv_wait(j, o_away)
    attend(o_away, -3 * sigma)
    for j in range(blocks):
        kv_wait(j, o_far)
    attend(o_far, 3 * sigma)

    ab[t] = (o_s[...] / l_s[0:1, :]).astype(BF16)

    def ab_send(slot, target):
        send(ab.at[slot], ab.at[slot], r_ab.at[slot], (q, target))

    def ab_wait(slot):
        arrived(ab.at[slot], r_ab.at[slot])

    for target in (tid(0, 1, 0), tid(2, 0, 0), tid(1, 0, 0), tid(3, 0, 0), other):
        ab_send(t, target)
    for k in range(1, 16):
        source = (t + k) % 16
        arrived(wo_recv.at[source], r_wo.at[source])
    wo_recv[t] = wo_send[t]
    slot = tid(0, 1, 0)
    ab_wait(slot)
    for target in (tid(1, 0, 0), tid(3, 0, 0), other):
        ab_send(slot, target)
    for dx in (1, 3):
        slot = tid(dx, 0, 0)
        ab_wait(slot)
        ab_send(slot, other)
    slot = tid(2, 0, 0)
    ab_wait(slot)
    ab_send(slot, tid(0, 1, 0))
    ab_send(slot, other)
    for dx in (1, 3, 2):
        slot = tid(dx, 1, 0)
        ab_wait(slot)
        ab_send(slot, other)
    for dx in range(4):
        for fy in range(2):
            ab_wait(tid(dx, fy, 1))

    def mix(k, total):
        weights = jnp.concatenate([wo_recv[2 * k], wo_recv[2 * k + 1]], axis=1)
        heads = ab[pl.ds(2 * k, 2)].reshape(2 * HD, blocks * LANE)
        return total + jnp.dot(weights, heads, preferred_element_type=F32)

    proj = lax.fori_loop(0, 8, mix, jnp.zeros((part, blocks * LANE), F32))
    for j in range(blocks):
        lanes = slice(j * LANE, (j + 1) * LANE)
        out_ref[:, lanes] = (xr[j].astype(F32) + modc[2] * proj[:, lanes]).astype(BF16)
    for copy in sends:
        copy.wait_send()


def local(frames_in, fresh, levels, reach, level_mod, w_qkv, q_gain, k_gain, w_out):
    queues = lax.axis_size("queue")
    tokens, part = fresh.shape
    model = w_qkv.shape[0]
    blocks = tokens // LANE
    vmem = pltpu.VMEM
    dma = pltpu.SemaphoreType.DMA
    any_spec = pl.BlockSpec(memory_space=pl.ANY)
    smem_spec = pl.BlockSpec(memory_space=pltpu.SMEM)
    out = pl.pallas_call(
        lambda *refs: kernel(queues, *refs),
        out_shape=jax.ShapeDtypeStruct((part, tokens), BF16),
        in_specs=[smem_spec, smem_spec] + [any_spec] * 7,
        out_specs=pl.BlockSpec(memory_space=pltpu.VMEM),
        scratch_shapes=[
            vmem((blocks, part, LANE), BF16),
            vmem((blocks, part, LANE), BF16),
            vmem((8, LANE), F32),
            vmem((16, 8, LANE), F32),
            vmem((3, part, LANE), BF16),
            vmem((3, part, 1), F32),
            vmem((3, model, LANE), BF16),
            vmem((8, 3 * HD, 2 * part), BF16),
            vmem((blocks, 16, part, LANE), BF16),
            vmem((HD, tokens), BF16),
            vmem((7, blocks, 2, HD, HD), BF16),
            vmem((8, tokens), F32),
            vmem((8, tokens), F32),
            vmem((HD, tokens), F32),
            vmem((16, HD, tokens), BF16),
            vmem((HD, model), BF16),
            vmem((16, part, HD), BF16),
            vmem((16, part, HD), BF16),
            vmem((16, LANE), F32),
            dma((16,)),
            dma((128,)),
            dma((blocks,)),
            dma((16,)),
            dma((blocks, 16)),
            dma((7, blocks)),
            dma((16,)),
            dma((16,)),
        ],
        compiler_params=pltpu.CompilerParams(
            collective_id=0, has_side_effects=True, vmem_limit_bytes=56 * 1024 * 1024
        ),
        name="block",
    )(
        levels, reach, frames_in[0].T, fresh.T, jnp.transpose(level_mod, (1, 2, 0)),
        jnp.transpose(w_qkv, (1, 0, 2)), q_gain.reshape(1, HD), k_gain.reshape(1, HD), w_out,
    )
    return out.T[None]


def solution(mesh):
    return jax.shard_map(
        local,
        mesh=mesh,
        in_specs=(
            P("queue", None, "tensor"),
            P(None, "tensor"),
            P("queue"),
            P("queue"),
            P(None, None, "tensor"),
            P(None, None, "tensor"),
            P("tensor"),
            P("tensor"),
            P("tensor", None),
        ),
        out_specs=P("queue", None, "tensor"),
        check_vma=False,
    )
```

time: 212 us -> 79.2 us (0.37)
  waiting for transfers between devices: 94.7 us -> 0 us
  Pallas kernels: 0 us -> 76.2 us
  starting transfers between devices: 61 us -> 0 us
  blocking collectives: 20.6 us -> 0 us
  between operations: 15.1 us -> 1.3 us
  other arithmetic: 8.53 us -> 0 us
  matrix products: 7.06 us -> 0 us
  local copies, waits for them, and re-layouts: 4.46 us -> 1.59 us
    pallas_call x0 -> x1, Pallas kernels: none -> 76.2 us  [local(): pl.pallas_call(lambda *refs: kernel(queues, *refs), out_shape=jax.ShapeDt...]
    all_gather x2 -> x0, waiting for transfers between devices: 48.7 us -> none  [the longest x1 26.2 us: local(): lax.all_gather(attn, 'tensor', axis=1, tiled=True)]
    ppermute x13 -> x0, starting transfers between devices: 48 us -> none  [passed_along(): lax.ppermute(value, axis, [(source, source + steps) for source in range(f...]
    ppermute x13 -> x0, waiting for transfers between devices: 33.3 us -> none  [passed_along(): lax.ppermute(value, axis, [(source, source + steps) for source in range(f...]
    all_gather x1 -> x0, blocking collectives: 20.6 us -> none  [local(): lax.all_gather(picked_half[:2], 'tensor', axis=1, tiled=True)]
    all_to_all x1 -> x0, starting transfers between devices: 13 us -> none  [local(): lax.all_to_all(w_out, 'tensor', split_axis=1, concat_axis=0, tiled=True)]
    all_to_all x1 -> x0, waiting for transfers between devices: 12.6 us -> none  [local(): lax.all_to_all(w_out, 'tensor', split_axis=1, concat_axis=0, tiled=True)]
    dot_general x4 -> x0, matrix products: 7.06 us -> none  [the longest x1 2.74 us: local(): jnp.dot(lax.all_gather(attn, 'tensor', axis=1, tiled=True), head_rows, pr...]
  transfers between devices with their start and end apart: 16 -> 0, of which waited for: 11 -> 0; matrix products, arithmetic and copies ran while one was open for 4% -> 0% of each run, Pallas kernels for 0% -> 0%
where the time goes in v1:
time: 79.2 us; the launch traced here: 79.1 us
  Pallas kernels  76.2 us (96%)
  local copies, waits for them, and re-layouts  1.59 us (2%)
  between operations  1.3 us (2%)
    pallas_call x1, Pallas kernels, local(): pl.pallas_call(lambda *refs: kernel(queues, *refs), out_shape=jax.ShapeDt...  76.2 us
    unnamed x1, local copies, waits for them, and re-layouts  1.59 us

profile of v1, /device:TPU:1, one launch (start us, length us, event | category | flops | bytes accessed | tf_op | source)
XLA Modules:
  0.0 79.1 jit_solution(15227467147070289985)
XLA Ops:
  1.3 76.2 %block.1 = bf16[192,384]{1,0:T(8,128)(2,1)} custom-call(s32[1]{0:T(128)S(6)} %copy.11.refs_0_, s32[1]{0:T(128)S(6)} %copy.12.refs_1_, bf16[192,384]{1,0:T(8,128)(2,1)} %bitcast.13, bf16[192,384]{1,0:T(8,128)(2,1)} %bitcast.14, bf16[3,192,128]{2,1,0:T(8,128)(2,1)} %bitcast.15, bf16[3,3072,128]{2,1,0:T(8,128)(2,1)} %bitcast.11, f32[1,128]{1,0:T(1,128)} %bitcast.16, ...), custom_call_target="tpu_custom_call" | custom-call | tf_op jit(solution)/shard_map/block/pallas_call | solution.py:349
  77.5 1.6 %copy.13 = bf16[1,384,192]{1,2,0:T(8,128)(2,1)} copy(bf16[1,384,192]{1,2,0:T(8,128)(2,1)} %bitcast.12) | data formatting | bytes 294912

commit v2 on v1

--- a/solution.py
+++ b/solution.py
@@ -17,7 +17,7 @@
     queues, levels_ref, reach_ref, frames_ref, fresh_ref, mod_ref, w_ref, qg_ref, kg_ref, wo_ref,
     out_ref,
     xs, xr, st, stb, lm, modc, wq, wt, hb, qt, kv, m_s, l_s, o_s, ab, wo_in, wo_send, wo_recv, gains,
-    local_sem, ss, r_shift, r_stat, r_h, r_kv, r_ab, r_wo,
+    level_s, reach_s, local_sem, ss, r_shift, r_stat, r_h, r_kv, r_ab, r_wo,
 ):
     blocks = xs.shape[0]
     part = xs.shape[1]
@@ -74,12 +74,14 @@
         def _():
             from_queue.start()
 
+    load_wo = load(wo_ref, wo_in)
+    load_level = load(levels_ref, level_s)
+    load_reach = load(reach_ref, reach_s)
     load_mod = load(mod_ref, lm)
     load_w = load(w_ref, wq)
-    load_wo = load(wo_ref, wo_in)
     load_qg = load(qg_ref, gains.at[pl.ds(0, 1)])
     load_kg = load(kg_ref, gains.at[pl.ds(8, 1)])
-    for copy in (load_mod, load_w, load_wo, load_qg, load_kg):
+    for copy in loads[blocks:]:
         copy.start()
 
     after = (q + 1) % queues
@@ -92,6 +94,8 @@
         pl.semaphore_signal(barrier, inc=1, device_id=(before, (t + k) % 16), device_id_type=MESH)
     for dz in (1, -1):
         pl.semaphore_signal(barrier, inc=1, device_id=(queue_id(dz, 0), t), device_id_type=MESH)
+    sigma = 2 * e - 1
+    pl.semaphore_signal(barrier, inc=1, device_id=(queue_id(2 * sigma, 1), t), device_id_type=MESH)
 
     for j in range(blocks):
         loads[j].wait()
@@ -100,7 +104,7 @@
         rest = values - total * (1.0 / part)
         st[j : j + 1, :] = total
         st[blocks + j : blocks + j + 1, :] = jnp.sum(rest * rest, axis=0, keepdims=True)
-    pl.semaphore_wait(barrier, 15 + 32 + 2)
+    pl.semaphore_wait(barrier, 15 + 32 + 3)
 
     send(xs.at[0], xr.at[0], r_shift.at[0], (after, t))
     for k in range(16):
@@ -108,8 +112,31 @@
     for j in range(1, blocks):
         send(xs.at[j], xr.at[j], r_shift.at[j], (after, t))
 
+    load_wo.wait()
+
+    def turn_out(k, _):
+        lanes = pl.ds(pl.multiple_of(k * 384, 128), 384)
+        wo_send[pl.ds(2 * k, 2)] = wo_in[:, lanes].T.reshape(2, part, LANE)
+        return 0
+
+    lax.fori_loop(0, 8, turn_out, 0)
+
+    def send_out(across, steps):
+        for dx in steps:
+            for fc in range(2):
+                if across:
+                    target = tid(dx, 1, fc)
+                    send(wo_send.at[target], wo_recv.at[t], r_wo.at[t], (queue_id(0, fc), target))
+                elif dx or fc:
+                    target = tid(dx, 0, fc)
+                    send(wo_send.at[target], wo_recv.at[t], r_wo.at[t], (q, target))
+
+    send_out(False, (2, 1, 3, 0))
+
+    load_level.wait()
+    load_reach.wait()
     load_mod.wait()
-    chosen = lax.broadcasted_iota(jnp.int32, (part, LANE), 1) == levels_ref[0]
+    chosen = lax.broadcasted_iota(jnp.int32, (part, LANE), 1) == level_s[0]
     for k in range(3):
         modc[k] = jnp.sum(jnp.where(chosen, lm[k].astype(F32), 0.0), axis=1, keepdims=True)
     load_qg.wait()
@@ -129,11 +156,44 @@
 
     lax.fori_loop(0, 8, turn, 0)
 
-    def slot_wait(j, slot):
-        arrived(hb.at[j, slot], r_h.at[j, slot])
-
-    def slot_send(j, slot, device_t):
-        send(hb.at[j, slot], hb.at[j, slot], r_h.at[j, slot], (q, device_t))
+    def slot_wait(buf, sems, j, slot):
+        arrived(buf.at[j, slot], sems.at[j, slot])
+
+    def slot_send(buf, sems, j, slot, device_t):
+        send(buf.at[j, slot], buf.at[j, slot], sems.at[j, slot], (q, device_t))
+
+    other = tid(0, 0, 1)
+    order = ((0, 0), (0, 1), (1, 0), (3, 0), (2, 0), (1, 1), (3, 1), (2, 1))
+
+    def gather_own(buf, sems, j):
+        for target in (tid(0, 1, 0), tid(2, 0, 0), tid(1, 0, 0), tid(3, 0, 0), other):
+            slot_send(buf, sems, j, t, target)
+
+    def relay_y(buf, sems, j):
+        slot = tid(0, 1, 0)
+        slot_wait(buf, sems, j, slot)
+        for target in (tid(1, 0, 0), tid(3, 0, 0), other):
+            slot_send(buf, sems, j, slot, target)
+
+    def relay_far(buf, sems, j):
+        slot = tid(2, 0, 0)
+        slot_wait(buf, sems, j, slot)
+        slot_send(buf, sems, j, slot, tid(0, 1, 0))
+        slot_send(buf, sems, j, slot, other)
+
+    def relay_chip(buf, sems, j, dx, fy):
+        slot = tid(dx, fy, 0)
+        slot_wait(buf, sems, j, slot)
+        slot_send(buf, sems, j, slot, other)
+
+    def relay_sides(buf, sems, j):
+        relay_chip(buf, sems, j, 1, 0)
+        relay_chip(buf, sems, j, 3, 0)
+
+    def late(buf, sems, j):
+        relay_chip(buf, sems, j, 1, 1)
+        relay_chip(buf, sems, j, 3, 1)
+        relay_chip(buf, sems, j, 2, 1)
 
     for k in range(16):
         slot = (t + k) % 16
@@ -147,40 +207,8 @@
         arrived(xr.at[j], r_shift.at[j])
         normed = (xr[j].astype(F32) - center[j : j + 1, :]) * factor[j : j + 1, :]
         hb[j, t] = (normed * (1.0 + modc[1]) + modc[0]).astype(BF16)
-        for target in (tid(0, 1, 0), tid(2, 0, 0), tid(1, 0, 0), tid(3, 0, 0), tid(0, 0, 1)):
-            slot_send(j, t, target)
-
-    other = tid(0, 0, 1)
-
-    def relay_y(j):
-        slot = tid(0, 1, 0)
-        slot_wait(j, slot)
-        for target in (tid(1, 0, 0), tid(3, 0, 0), other):
-            slot_send(j, slot, target)
-
-    def relay_far(j):
-        slot = tid(2, 0, 0)
-        slot_wait(j, slot)
-        slot_send(j, slot, tid(0, 1, 0))
-        slot_send(j, slot, other)
-
-    def relay_chip(j, dx, fy):
-        slot = tid(dx, fy, 0)
-        slot_wait(j, slot)
-        slot_send(j, slot, other)
-
-    def early(j):
-        relay_y(j)
-        relay_chip(j, 1, 0)
-        relay_chip(j, 3, 0)
-        relay_far(j)
-
-    def late(j):
-        relay_chip(j, 1, 1)
-        relay_chip(j, 3, 1)
-        relay_chip(j, 2, 1)
-
-    sigma = 2 * e - 1
+        gather_own(hb, r_h, j)
+
     own, s_near, s_away, o_0, o_near, o_away, o_far = range(7)
 
     def kv_send(j, slot, there, device):
@@ -190,16 +218,14 @@
         arrived(kv.at[slot, j], r_kv.at[slot, j])
 
     def project(j):
-        for dx in range(4):
-            for fy in range(2):
-                slot = tid(dx, fy, 1)
-                slot_wait(j, slot)
-
         def one(chip, total):
             h = hb[j, pl.ds(2 * chip, 2)].reshape(2 * part, LANE)
             return total + jnp.dot(wt[chip], h, preferred_element_type=F32)
 
-        packed = lax.fori_loop(0, 8, one, jnp.zeros((3 * HD, LANE), F32))
+        packed = jnp.zeros((3 * HD, LANE), F32)
+        for dx, fy in order:
+            slot_wait(hb, r_h, j, tid(dx, fy, 1))
+            packed = one(tid(dx, fy, 0) // 2, packed)
         query, keyed, valued = packed[:HD], packed[HD : 2 * HD], packed[2 * HD :]
 
         def rms(values, gain):
@@ -210,6 +236,8 @@
         kv[own, j, 1] = valued.astype(BF16)
         kv_send(j, own, s_near, (queue_id(sigma, 0), t))
         kv_send(j, own, o_0, (queue_id(0, 1), t))
+        if j == blocks - 1:
+            kv_send(j, own, o_far, (queue_id(2 * sigma, 1), t))
         kv_send(j, own, s_away, (queue_id(-sigma, 0), t))
         qt[:, j * LANE : (j + 1) * LANE] = rms(query, q_gain)
 
@@ -225,29 +253,25 @@
 
     normalise(0)
     normalise(1)
-    early(0)
+    relay_y(hb, r_h, 0)
     normalise(2)
-    early(1)
-    late(0)
+    relay_far(hb, r_h, 0)
+    relay_y(hb, r_h, 1)
+    relay_sides(hb, r_h, 0)
+    relay_far(hb, r_h, 1)
+    relay_y(hb, r_h, 2)
+    relay_sides(hb, r_h, 1)
+    late(hb, r_h, 0)
+    relay_far(hb, r_h, 2)
     project(0)
-    early(2)
-    late(1)
+    relay_sides(hb, r_h, 2)
+    late(hb, r_h, 1)
     project(1)
     kv_relay_1(0)
-    late(2)
+    late(hb, r_h, 2)
     project(2)
-
-    load_wo.wait()
-
-    def turn_out(k, _):
-        lanes = pl.ds(pl.multiple_of(k * 384, 128), 384)
-        wo_send[pl.ds(2 * k, 2)] = wo_in[:, lanes].T.reshape(2, part, LANE)
-        return 0
-
-    lax.fori_loop(0, 8, turn_out, 0)
-    for k in range(1, 16):
-        target = (t + k) % 16
-        send(wo_send.at[target], wo_recv.at[t], r_wo.at[t], (q, target))
+    kv_relay_1(1)
+    kv_relay_2(0)
 
     f = q
     scale = HD ** (-0.5)
@@ -255,84 +279,82 @@
     l_s[...] = jnp.zeros(l_s.shape, F32)
     o_s[...] = jnp.zeros(o_s.shape, F32)
 
-    def attend(slot, offset):
+    def attend(slot, offset, span=(0, 3)):
+        lanes = slice(span[0] * LANE, span[1] * LANE)
         keys = kv[slot, :, 0].reshape(blocks * LANE, HD)
-        scores = jnp.dot(keys, qt[...], preferred_element_type=F32)
+        scores = jnp.dot(keys, qt[:, lanes], preferred_element_type=F32)
         frame = f + offset
-        usable = (jnp.abs(offset) <= reach_ref[0]) & (frame >= 0) & (frame < queues)
+        usable = (jnp.abs(offset) <= reach_s[0]) & (frame >= 0) & (frame < queues)
         scores = scores * scale + jnp.where(usable, 0.0, -jnp.inf).astype(F32)
-        m_old = m_s[0:1, :]
+        m_old = m_s[0:1, lanes]
         m_new = jnp.maximum(m_old, jnp.max(scores, axis=0, keepdims=True))
         weights = jnp.exp(scores - m_new)
         fade = jnp.exp(m_old - m_new)
-        l_s[0:1, :] = l_s[0:1, :] * fade + jnp.sum(weights, axis=0, keepdims=True)
-        m_s[0:1, :] = m_new
+        l_s[0:1, lanes] = l_s[0:1, lanes] * fade + jnp.sum(weights, axis=0, keepdims=True)
+        m_s[0:1, lanes] = m_new
         half = weights.astype(BF16)
         values = jnp.concatenate([kv[slot, j, 1] for j in range(blocks)], axis=1)
-        o_s[...] = o_s[...] * fade + jnp.dot(values, half, preferred_element_type=F32)
-
-    kv_relay_1(1)
-    kv_relay_2(0)
+        o_s[:, lanes] = o_s[:, lanes] * fade + jnp.dot(values, half, preferred_element_type=F32)
+
     attend(own, 0)
     kv_relay_1(2)
     kv_relay_2(1)
+    send_out(True, (2, 1, 3, 0))
     attend(s_near, -2 * sigma)
     attend(o_0, -sigma)
-    kv_relay_2(2)
+    for slot, offset in ((s_away, 2 * sigma), (o_far, 3 * sigma)):
+        for j in range(blocks):
+            kv_wait(j, slot)
+        attend(slot, offset)
+    kv_wait(blocks - 1, o_near)
     attend(o_near, sigma)
     for j in range(blocks):
-        kv_wait(j, s_away)
-    attend(s_away, 2 * sigma)
-    for j in range(blocks):
         kv_wait(j, o_away)
-    attend(o_away, -3 * sigma)
-    for j in range(blocks):
-        kv_wait(j, o_far)
-    attend(o_far, 3 * sigma)
-
-    ab[t] = (o_s[...] / l_s[0:1, :]).astype(BF16)
-
-    def ab_send(slot, target):
-        send(ab.at[slot], ab.at[slot], r_ab.at[slot], (q, target))
-
-    def ab_wait(slot):
-        arrived(ab.at[slot], r_ab.at[slot])
-
-    for target in (tid(0, 1, 0), tid(2, 0, 0), tid(1, 0, 0), tid(3, 0, 0), other):
-        ab_send(t, target)
-    for k in range(1, 16):
-        source = (t + k) % 16
-        arrived(wo_recv.at[source], r_wo.at[source])
+
+    def finish(j):
+        attend(o_away, -3 * sigma, (j, j + 1))
+        lanes = slice(j * LANE, (j + 1) * LANE)
+        ab[j, t] = (o_s[:, lanes] / l_s[0:1, lanes]).astype(BF16)
+        gather_own(ab, r_ab, j)
+
+    def out_wait(dx, fy, fc):
+        if dx or fy or fc:
+            source = tid(dx, fy, fc)
+            arrived(wo_recv.at[source], r_wo.at[source])
+
+    def mix(j):
+        total = jnp.zeros((part, LANE), F32)
+        for dx, fy in order:
+            slot_wait(ab, r_ab, j, tid(dx, fy, 1))
+            if j == 0:
+                out_wait(dx, fy, 0)
+                out_wait(dx, fy, 1)
+            k = tid(dx, fy, 0) // 2
+            weights = jnp.concatenate([wo_recv[2 * k], wo_recv[2 * k + 1]], axis=1)
+            heads = ab[j, pl.ds(2 * k, 2)].reshape(2 * HD, LANE)
+            total = total + jnp.dot(weights, heads, preferred_element_type=F32)
+        lanes = slice(j * LANE, (j + 1) * LANE)
+        out_ref[:, lanes] = (xr[j].astype(F32) + modc[2] * total).astype(BF16)
+
     wo_recv[t] = wo_send[t]
-    slot = tid(0, 1, 0)
-    ab_wait(slot)
-    for target in (tid(1, 0, 0), tid(3, 0, 0), other):
-        ab_send(slot, target)
-    for dx in (1, 3):
-        slot = tid(dx, 0, 0)
-        ab_wait(slot)
-        ab_send(slot, other)
-    slot = tid(2, 0, 0)
-    ab_wait(slot)
-    ab_send(slot, tid(0, 1, 0))
-    ab_send(slot, other)
-    for dx in (1, 3, 2):
-        slot = tid(dx, 1, 0)
-        ab_wait(slot)
-        ab_send(slot, other)
-    for dx in range(4):
-        for fy in range(2):
-            ab_wait(tid(dx, fy, 1))
-
-    def mix(k, total):
-        weights = jnp.concatenate([wo_recv[2 * k], wo_recv[2 * k + 1]], axis=1)
-        heads = ab[pl.ds(2 * k, 2)].reshape(2 * HD, blocks * LANE)
-        return total + jnp.dot(weights, heads, preferred_element_type=F32)
-
-    proj = lax.fori_loop(0, 8, mix, jnp.zeros((part, blocks * LANE), F32))
-    for j in range(blocks):
-        lanes = slice(j * LANE, (j + 1) * LANE)
-        out_ref[:, lanes] = (xr[j].astype(F32) + modc[2] * proj[:, lanes]).astype(BF16)
+    finish(0)
+    finish(1)
+    finish(2)
+    relay_y(ab, r_ab, 0)
+    relay_y(ab, r_ab, 1)
+    relay_y(ab, r_ab, 2)
+    relay_far(ab, r_ab, 0)
+    relay_sides(ab, r_ab, 0)
+    relay_far(ab, r_ab, 1)
+    relay_sides(ab, r_ab, 1)
+    relay_far(ab, r_ab, 2)
+    relay_sides(ab, r_ab, 2)
+    late(ab, r_ab, 0)
+    mix(0)
+    late(ab, r_ab, 1)
+    mix(1)
+    late(ab, r_ab, 2)
+    mix(2)
     for copy in sends:
         copy.wait_send()
 
@@ -345,11 +367,10 @@
     vmem = pltpu.VMEM
     dma = pltpu.SemaphoreType.DMA
     any_spec = pl.BlockSpec(memory_space=pl.ANY)
-    smem_spec = pl.BlockSpec(memory_space=pltpu.SMEM)
     out = pl.pallas_call(
         lambda *refs: kernel(queues, *refs),
         out_shape=jax.ShapeDtypeStruct((part, tokens), BF16),
-        in_specs=[smem_spec, smem_spec] + [any_spec] * 7,
+        in_specs=[pl.BlockSpec(memory_space=pltpu.HBM)] * 2 + [any_spec] * 7,
         out_specs=pl.BlockSpec(memory_space=pltpu.VMEM),
         scratch_shapes=[
             vmem((blocks, part, LANE), BF16),
@@ -366,18 +387,20 @@
             vmem((8, tokens), F32),
             vmem((8, tokens), F32),
             vmem((HD, tokens), F32),
-            vmem((16, HD, tokens), BF16),
+            vmem((blocks, 16, HD, LANE), BF16),
             vmem((HD, model), BF16),
             vmem((16, part, HD), BF16),
             vmem((16, part, HD), BF16),
             vmem((16, LANE), F32),
+            pltpu.SMEM((1,), jnp.int32),
+            pltpu.SMEM((1,), jnp.int32),
             dma((16,)),
-            dma((128,)),
+            dma((160,)),
             dma((blocks,)),
             dma((16,)),
             dma((blocks, 16)),
             dma((7, blocks)),
-            dma((16,)),
+            dma((blocks, 16)),
             dma((16,)),
         ],
         compiler_params=pltpu.CompilerParams(

time: 79.2 us -> 71.2 us (0.90)
  Pallas kernels: 76.2 us -> 68.2 us
    pallas_call x1, Pallas kernels: 76.2 us -> 68.2 us  [local(): pl.pallas_call(lambda *refs: kernel(queues, *refs), out_shape=jax.ShapeDt...]
where the time goes in v2:
time: 71.2 us; the launch traced here: 71.1 us
  Pallas kernels  68.2 us (96%)
  local copies, waits for them, and re-layouts  1.59 us (2%)
  between operations  1.3 us (2%)
    pallas_call x1, Pallas kernels, local(): pl.pallas_call(lambda *refs: kernel(queues, *refs), out_shape=jax.ShapeDt...  68.2 us
    unnamed x1, local copies, waits for them, and re-layouts  1.59 us

profile of v2, /device:TPU:1, one launch (start us, length us, event | category | flops | bytes accessed | tf_op | source)
XLA Modules:
  0.0 71.1 jit_solution(6158618811360749808)
XLA Ops:
  1.3 68.2 %block.1 = bf16[192,384]{1,0:T(8,128)(2,1)} custom-call(s32[1]{0:T(128)S(6)} %copy.11.refs_0_, s32[1]{0:T(128)S(6)} %copy.12.refs_1_, bf16[192,384]{1,0:T(8,128)(2,1)} %bitcast.13, bf16[192,384]{1,0:T(8,128)(2,1)} %bitcast.14, bf16[3,192,128]{2,1,0:T(8,128)(2,1)} %bitcast.15, bf16[3,3072,128]{2,1,0:T(8,128)(2,1)} %bitcast.11, f32[1,128]{1,0:T(1,128)} %bitcast.16, ...), custom_call_target="tpu_custom_call" | custom-call | tf_op jit(solution)/shard_map/block/pallas_call | solution.py:370
  69.5 1.6 %copy.13 = bf16[1,384,192]{1,2,0:T(8,128)(2,1)} copy(bf16[1,384,192]{1,2,0:T(8,128)(2,1)} %bitcast.12) | data formatting | bytes 294912

commit v3 on v2

--- a/solution.py
+++ b/solution.py
@@ -234,17 +234,16 @@
 
         kv[own, j, 0] = rms(keyed, k_gain).T
         kv[own, j, 1] = valued.astype(BF16)
-        kv_send(j, own, s_near, (queue_id(sigma, 0), t))
         kv_send(j, own, o_0, (queue_id(0, 1), t))
         if j == blocks - 1:
             kv_send(j, own, o_far, (queue_id(2 * sigma, 1), t))
+        kv_send(j, own, s_near, (queue_id(sigma, 0), t))
         kv_send(j, own, s_away, (queue_id(-sigma, 0), t))
         qt[:, j * LANE : (j + 1) * LANE] = rms(query, q_gain)
 
     def kv_relay_1(j):
-        kv_wait(j, s_near)
-        kv_send(j, s_near, o_near, (queue_id(0, 1), t))
         kv_wait(j, o_0)
+        kv_send(j, o_0, o_near, (queue_id(-sigma, 0), t))
         kv_send(j, o_0, o_away, (queue_id(sigma, 0), t))
 
     def kv_relay_2(j):
@@ -300,9 +299,8 @@
     kv_relay_1(2)
     kv_relay_2(1)
     send_out(True, (2, 1, 3, 0))
-    attend(s_near, -2 * sigma)
     attend(o_0, -sigma)
-    for slot, offset in ((s_away, 2 * sigma), (o_far, 3 * sigma)):
+    for slot, offset in ((s_near, -2 * sigma), (s_away, 2 * sigma), (o_far, 3 * sigma)):
         for j in range(blocks):
             kv_wait(j, slot)
         attend(slot, offset)
@@ -369,7 +367,7 @@
     any_spec = pl.BlockSpec(memory_space=pl.ANY)
     out = pl.pallas_call(
         lambda *refs: kernel(queues, *refs),
-        out_shape=jax.ShapeDtypeStruct((part, tokens), BF16),
+        out_shape=pltpu.VMEM((part, tokens), BF16),
         in_specs=[pl.BlockSpec(memory_space=pltpu.HBM)] * 2 + [any_spec] * 7,
         out_specs=pl.BlockSpec(memory_space=pltpu.VMEM),
         scratch_shapes=[

time: 71.2 us -> 68.1 us (0.956)
  Pallas kernels: 68.2 us -> 65.9 us
  local copies, waits for them, and re-layouts: 1.59 us -> 0.66 us
    pallas_call x1, Pallas kernels: 68.2 us -> 65.9 us  [local(): pl.pallas_call(lambda *refs: kernel(queues, *refs), out_shape=pltpu.VMEM(...]
    unnamed x1, local copies, waits for them, and re-layouts: 1.59 us -> 0.66 us
where the time goes in v3:
time: 68.1 us; the launch traced here: 67.9 us
  Pallas kernels  65.9 us (97%)
  between operations  1.3 us (2%)
    pallas_call x1, Pallas kernels, local(): pl.pallas_call(lambda *refs: kernel(queues, *refs), out_shape=pltpu.VMEM(...  65.9 us

profile of v3, /device:TPU:1, one launch (start us, length us, event | category | flops | bytes accessed | tf_op | source)
XLA Modules:
  0.0 67.9 jit_solution(1570581350970988139)
XLA Ops:
  1.3 65.9 %block.1 = bf16[192,384]{1,0:T(8,128)(2,1)S(1)} custom-call(s32[1]{0:T(128)S(6)} %copy.12.refs_0_, s32[1]{0:T(128)S(6)} %copy.13.refs_1_, bf16[192,384]{1,0:T(8,128)(2,1)} %bitcast.13, bf16[192,384]{1,0:T(8,128)(2,1)} %bitcast.14, bf16[3,192,128]{2,1,0:T(8,128)(2,1)} %bitcast.15, bf16[3,3072,128]{2,1,0:T(8,128)(2,1)} %bitcast.12, f32[1,128]{1,0:T(1,128)} %bitcast.16, ...), custom_call_target="tpu_custom_call" | custom-call | tf_op jit(solution)/shard_map/block/pallas_call | solution.py:368
  67.2 0.7 copy.11

commit v4 on v3

--- a/solution.py
+++ b/solution.py
@@ -106,9 +106,9 @@
         st[blocks + j : blocks + j + 1, :] = jnp.sum(rest * rest, axis=0, keepdims=True)
     pl.semaphore_wait(barrier, 15 + 32 + 3)
 
-    send(xs.at[0], xr.at[0], r_shift.at[0], (after, t))
     for k in range(16):
         send(st, stb.at[t], r_stat.at[t], (after, (t + k) % 16))
+    send(xs.at[0], xr.at[0], r_shift.at[0], (after, t))
     for j in range(1, blocks):
         send(xs.at[j], xr.at[j], r_shift.at[j], (after, t))
 
@@ -266,8 +266,8 @@
     relay_sides(hb, r_h, 2)
     late(hb, r_h, 1)
     project(1)
+    late(hb, r_h, 2)
     kv_relay_1(0)
-    late(hb, r_h, 2)
     project(2)
     kv_relay_1(1)
     kv_relay_2(0)

time: 68.1 us -> 67.1 us (0.985)
  Pallas kernels: 65.9 us -> 65 us
    pallas_call x1, Pallas kernels: 65.9 us -> 65 us  [local(): pl.pallas_call(lambda *refs: kernel(queues, *refs), out_shape=pltpu.VMEM(...]
where the time goes in v4:
time: 67.1 us; the launch traced here: 66.9 us
  Pallas kernels  65 us (97%)
  between operations  1.3 us (2%)
    pallas_call x1, Pallas kernels, local(): pl.pallas_call(lambda *refs: kernel(queues, *refs), out_shape=pltpu.VMEM(...  65 us

profile of v4, /device:TPU:1, one launch (start us, length us, event | category | flops | bytes accessed | tf_op | source)
XLA Modules:
  0.0 66.9 jit_solution(1665413650473143679)
XLA Ops:
  1.3 65.0 %block.1 = bf16[192,384]{1,0:T(8,128)(2,1)S(1)} custom-call(s32[1]{0:T(128)S(6)} %copy.12.refs_0_, s32[1]{0:T(128)S(6)} %copy.13.refs_1_, bf16[192,384]{1,0:T(8,128)(2,1)} %bitcast.13, bf16[192,384]{1,0:T(8,128)(2,1)} %bitcast.14, bf16[3,192,128]{2,1,0:T(8,128)(2,1)} %bitcast.15, bf16[3,3072,128]{2,1,0:T(8,128)(2,1)} %bitcast.12, f32[1,128]{1,0:T(1,128)} %bitcast.16, ...), custom_call_target="tpu_custom_call" | custom-call | tf_op jit(solution)/shard_map/block/pallas_call | solution.py:368
  66.3 0.7 copy.11

commit v5 on v4

--- a/solution.py
+++ b/solution.py
@@ -269,8 +269,6 @@
     late(hb, r_h, 2)
     kv_relay_1(0)
     project(2)
-    kv_relay_1(1)
-    kv_relay_2(0)
 
     f = q
     scale = HD ** (-0.5)
@@ -296,6 +294,8 @@
         o_s[:, lanes] = o_s[:, lanes] * fade + jnp.dot(values, half, preferred_element_type=F32)
 
     attend(own, 0)
+    kv_relay_1(1)
+    kv_relay_2(0)
     kv_relay_1(2)
     kv_relay_2(1)
     send_out(True, (2, 1, 3, 0))

time: 67.1 us -> 67.1 us (level)
  no operation moved by 1% of the time
where the time goes in v5:
time: 67.1 us; the launch traced here: 66.9 us
  Pallas kernels  65 us (97%)
  between operations  1.3 us (2%)
    pallas_call x1, Pallas kernels, local(): pl.pallas_call(lambda *refs: kernel(queues, *refs), out_shape=pltpu.VMEM(...  65 us

profile of v5, /device:TPU:1, one launch (start us, length us, event | category | flops | bytes accessed | tf_op | source)
XLA Modules:
  0.0 66.9 jit_solution(5302364669148915527)
XLA Ops:
  1.3 65.0 %block.1 = bf16[192,384]{1,0:T(8,128)(2,1)S(1)} custom-call(s32[1]{0:T(128)S(6)} %copy.12.refs_0_, s32[1]{0:T(128)S(6)} %copy.13.refs_1_, bf16[192,384]{1,0:T(8,128)(2,1)} %bitcast.13, bf16[192,384]{1,0:T(8,128)(2,1)} %bitcast.14, bf16[3,192,128]{2,1,0:T(8,128)(2,1)} %bitcast.15, bf16[3,3072,128]{2,1,0:T(8,128)(2,1)} %bitcast.12, f32[1,128]{1,0:T(1,128)} %bitcast.16, ...), custom_call_target="tpu_custom_call" | custom-call | tf_op jit(solution)/shard_map/block/pallas_call | solution.py:368
  66.3 0.7 copy.11
